TPU v7x, 32 devices: a whole 2x2x4 slice. The times are simulated.
32 devices in a mesh: ctx: 16 (over z, x, core), head: 2 (over y).
Axes of the slice: x: 2, y: 2, z: 4, core: 2. Of those that a mesh axis runs over, the one named last changes fastest.
Arguments:
- queries: bfloat16 [4096, 24, 128], P('ctx', 'head'), may hold values from -4.5 to 4.5, as said below
- key_vectors: bfloat16 [4096, 24, 128], P('ctx', 'head'), may hold values from -4.5 to 4.5, as said below
- value_vectors: bfloat16 [4096, 24, 128], P('ctx', 'head'), may hold values from -6 to 6
- attn_output: bfloat16 [4096, 24, 128], P('ctx', 'head'), may hold values from -6 to 6
- output_grad: bfloat16 [4096, 5120], P('ctx', 'head'), may hold values from -6 to 6
- w_out: bfloat16 [3072, 5120], P('head'), may hold values from -0.078125 to 0.078125
- log_total: float32 [4096, 24], P('ctx', 'head'), as said below
Outputs:
- query_grad: bfloat16 [4096, 24, 128], P('ctx', 'head')
- key_grad: bfloat16 [4096, 24, 128], P('ctx', 'head')
- value_grad: bfloat16 [4096, 24, 128], P('ctx', 'head')
Inputs may be any that keep to these rules, and one draw needn't show every extreme that they name: `queries`: independent entries of order one. `key_vectors`: entries of order one. `log_total`: for each position and head, the log of the sum of exp(scores) over the positions it sees, from the given queries and keys.
All inputs are finite; a program needn't handle non-finite values.
Results may differ from a plain program's by a relative error of at most 0.0058.
Values may be sent and summed in bfloat16 or wider, within the bound.
No kernel may reach another device: no remote copies, remote signals or barrier semaphores. Data moves between devices by JAX's collectives and lax.ppermute only.
A program may use at most 128 MiB of HBM per device.

v0:
```python
import jax
import jax.numpy as jnp
from jax import lax
from jax.sharding import PartitionSpec as P


def block_terms(
    query_block,
    grad_block,
    total_block,
    delta_block,
    key_block,
    value_block,
    query_pos,
    key_pos,
    factor,
):
    raw_scores = (
        jnp.einsum("qhd,khd->hqk", query_block, key_block, preferred_element_type=jnp.float32)
        * factor
    )
    visible = key_pos[None, None, :] <= query_pos[None, :, None]
    scores = jnp.where(visible, raw_scores, -jnp.inf)
    prob_full = jnp.exp(scores - total_block[:, :, None])
    prob_grad = jnp.einsum(
        "qhd,khd->hqk", grad_block, value_block, preferred_element_type=jnp.float32
    )
    score_grad = (prob_full * (prob_grad - delta_block[:, :, None])).astype(jnp.bfloat16)
    return (prob_full.astype(jnp.bfloat16), score_grad)


def query_pass(query_group, gathered_keys, gathered_values, span_rows, factor):
    query_rows, grad_rows, total_rows, delta_rows, query_pos = query_group
    highest = jnp.max(query_pos)

    def query_advance(step_index, running):
        offset = step_index * span_rows

        def query_update(query_grad):
            key_block = lax.dynamic_slice_in_dim(gathered_keys, offset, span_rows, 0)
            value_block = lax.dynamic_slice_in_dim(gathered_values, offset, span_rows, 0)
            key_pos = offset + jnp.arange(span_rows, dtype=jnp.int32)
            prob_low, score_grad = block_terms(
                query_rows,
                grad_rows,
                total_rows,
                delta_rows,
                key_block,
                value_block,
                query_pos,
                key_pos,
                factor,
            )
            return (
                query_grad
                + jnp.einsum(
                    "hqk,khd->qhd", score_grad, key_block, preferred_element_type=jnp.float32
                )
                * factor
            )

        return lax.cond(offset <= highest, query_update, lambda carried: carried, running)

    initial = jnp.zeros(query_rows.shape, jnp.float32)
    return lax.fori_loop(0, gathered_keys.shape[0] // span_rows, query_advance, initial)


def key_pass(
    own_keys, own_values, key_pos, all_queries, all_grads, all_totals, all_deltas, span_rows, factor
):
    lowest = jnp.min(key_pos)

    def key_advance(step_index, running):
        offset = step_index * span_rows

        def key_update(carried):
            key_grad, value_grad = carried
            query_block = lax.dynamic_slice_in_dim(all_queries, offset, span_rows, 0)
            grad_block = lax.dynamic_slice_in_dim(all_grads, offset, span_rows, 0)
            total_block = lax.dynamic_slice_in_dim(all_totals, offset, span_rows, 1)
            delta_block = lax.dynamic_slice_in_dim(all_deltas, offset, span_rows, 1)
            query_pos = offset + jnp.arange(span_rows, dtype=jnp.int32)
            prob_low, score_grad = block_terms(
                query_block,
                grad_block,
                total_block,
                delta_block,
                own_keys,
                own_values,
                query_pos,
                key_pos,
                factor,
            )
            key_grad = (
                key_grad
                + jnp.einsum(
                    "hqk,qhd->khd", score_grad, query_block, preferred_element_type=jnp.float32
                )
                * factor
            )
            value_grad = value_grad + jnp.einsum(
                "hqk,qhd->khd", prob_low, grad_block, preferred_element_type=jnp.float32
            )
            return (key_grad, value_grad)

        return lax.cond(
            offset + span_rows - 1 >= lowest, key_update, lambda carried: carried, running
        )

    initial = (jnp.zeros(own_keys.shape, jnp.float32), jnp.zeros(own_values.shape, jnp.float32))
    return lax.fori_loop(0, all_queries.shape[0] // span_rows, key_advance, initial)


def body(queries, key_vectors, value_vectors, attn_output, output_grad, w_out, log_total):
    local_rows, head_count, head_width = queries.shape
    factor = head_width ** (-0.5)
    ctx_count = lax.axis_size("ctx")
    ctx_index = lax.axis_index("ctx")
    total_len = local_rows * ctx_count
    span_rows = min(512, total_len)
    grad_flat = jnp.einsum(
        "tc,rc->tr",
        lax.all_gather(output_grad, "head", axis=1, tiled=True),
        w_out,
        preferred_element_type=jnp.float32,
    )
    attn_grad = grad_flat.astype(jnp.bfloat16).reshape(local_rows, head_count, head_width)
    row_delta = jnp.einsum(
        "qhd,qhd->hq", attn_grad, attn_output, preferred_element_type=jnp.float32
    )
    own_total = jnp.transpose(log_total, (1, 0))
    own_pos = ctx_index * local_rows + jnp.arange(local_rows, dtype=jnp.int32)
    groups = [(queries, attn_grad, own_total, row_delta, own_pos)]
    gathered_keys, gathered_values = (
        lax.all_gather(key_vectors, "ctx", axis=0, tiled=True),
        lax.all_gather(value_vectors, "ctx", axis=0, tiled=True),
    )
    partial_grads = [
        query_pass(query_group, gathered_keys, gathered_values, span_rows, factor)
        for query_group in groups
    ]
    all_queries, all_grads = (
        lax.all_gather(queries, "ctx", axis=0, tiled=True),
        lax.all_gather(attn_grad, "ctx", axis=0, tiled=True),
    )
    all_totals, all_deltas = (
        lax.all_gather(own_total, "ctx", axis=1, tiled=True),
        lax.all_gather(row_delta, "ctx", axis=1, tiled=True),
    )
    key_part, value_part = key_pass(
        key_vectors,
        value_vectors,
        own_pos,
        all_queries,
        all_grads,
        all_totals,
        all_deltas,
        span_rows,
        factor,
    )
    results = [piece.astype(jnp.bfloat16) for piece in partial_grads]
    query_grad = results[0]
    return (query_grad, key_part.astype(jnp.bfloat16), value_part.astype(jnp.bfloat16))


def solution(mesh):
    in_specs = (
        P("ctx", "head", None),
        P("ctx", "head", None),
        P("ctx", "head", None),
        P("ctx", "head", None),
        P("ctx", "head"),
        P("head", None),
        P("ctx", "head"),
    )
    out_specs = (P("ctx", "head", None), P("ctx", "head", None), P("ctx", "head", None))
    return jax.shard_map(body, mesh=mesh, in_specs=in_specs, out_specs=out_specs, check_vma=False)
```

profile of v0, /device:TPU:0, one launch (start us, length us, event | category | flops | bytes accessed | tf_op | source)
XLA Modules:
  0.0 605.7 jit_solution(5320497936110600833)
XLA Ops:
  9.4 41.9 %all-gather.10.cloned.1.call-done = bf16[256,5120]{1,0:T(8,128)(2,1)} async-done(((bf16[256,2560]{1,0:T(8,128)(2,1)}), bf16[256,5120]{1,0:T(8,128)(2,1)}) %all-gather.10.cloned.1.call-update) | async-done | bytes 2621456 | tf_op jit(solution)/shard_map/all_gather | solution.py:123
  51.3 10.5 %convolution_convert_fusion = bf16[256,1536]{1,0:T(8,128)(2,1)S(1)} fusion(bf16[256,5120]{1,0:T(8,128)(2,1)} %all-gather.10.cloned.1.call-done, bf16[1536,5120]{1,0:T(8,128)(2,1)} %param.20), kind=kOutput, calls=%fused_computation.52 | convolution fusion | flops 4026925056 | bytes 19136512 | tf_op jit(solution)/shard_map/tc,rc->tr/dot_general | solution.py:121
  64.9 24.9 %all_gather.25 = f32[12,4096]{1,0:T(8,128)} all-gather(f32[12,256]{1,0:T(8,128)S(1)} %bitcast.40), channel_id=1, replica_groups=mesh['ctx'=16,'head'=2] {'ctx'}, dimensions={1}, use_global_device_ids=true | all-gather | bytes 208896 | tf_op jit(solution)/shard_map/all_gather | solution.py:147
  94.4 20.7 %all_gather.27 = f32[12,4096]{1,0:T(8,128)} all-gather(f32[12,256]{1,0:T(8,128)S(1)} %multiply_reduce_fusion), channel_id=1, replica_groups=mesh['ctx'=16,'head'=2] {'ctx'}, dimensions={1}, use_global_device_ids=true | all-gather | bytes 208896 | tf_op jit(solution)/shard_map/all_gather | solution.py:148
  115.1 41.9 %all-gather.6.cloned.1.call-done = bf16[4096,12,128]{2,0,1:T(8,128)(2,1)} async-done(((bf16[256,12,128]{2,0,1:T(8,128)(2,1)}), bf16[4096,12,128]{2,0,1:T(8,128)(2,1)}) %all-gather.6.cloned.1.call-update) | async-done | bytes 12582928 | tf_op jit(solution)/shard_map/all_gather | solution.py:135
  156.9 101.7 %all-gather.8.cloned.1.call-done = bf16[4096,12,128]{2,0,1:T(8,128)(2,1)} async-done(((bf16[256,12,128]{2,0,1:T(8,128)(2,1)}), bf16[4096,12,128]{2,0,1:T(8,128)(2,1)}) %all-gather.8.cloned.1.call-update) | async-done | bytes 12582928 | tf_op jit(solution)/shard_map/all_gather | solution.py:136
  258.8 17.8 %while.37 = (s32[]{:T(128)}, f32[256,12,128]{0,2,1:T(8,128)S(1)}, s32[]{:T(128)}, bf16[4096,12,128]{2,0,1:T(8,128)(2,1)}, bf16[256,12,128]{2,0,1:T(8,128)(2,1)S(...) while((s32[]{:T(128)}, f32[256,12,128]{0,2,1:T(8,128)S(1)}, ...), condition=%wide.region_4.5_spmd.clone, body=%wide.region_1.4_spmd.clone.sunk | while | flops 1218315008 | bytes 22316308 | solution.py:65
  259.5 12.3 %conditional.6 = (f32[256,12,128]{0,2,1:T(8,128)S(1)}) conditional(s32[]{:T(128)} %convert_element_type.62, f32[256,12,128]{0,2,1:T(8,128)S(1)} %get-tuple-element.919, (s32[]{:T(128)}, bf16[4096,12,128]{2,0,1:T(8,128)(2,1)}, s32[]{:T(128)}, bf16[256,12,128]{2,0,1:T(8,128)(2,1)S(1)}, f32[12,256]{1,0:T(8,128)S(1)}, ...), branch_computations={%region_2.0_spmd, %region_3.3_spmd} | conditional | flops 1218315008 | bytes 22315062 | solution.py:62
  259.5 5.0 fusion.19
  264.7 7.1 %bitcast_add_fusion = f32[256,12,128]{0,2,1:T(8,128)S(1)} fusion(f32[256,12,128]{0,2,1:T(8,128)S(1)} %get-tuple-element.554, f32[12,512,256]{2,1,0:T(8,128)} %fusion.19, f32[12,256]{1,0:T(8,128)S(1)} %get-tuple-element.562, f32[12,256]{1,0:T(8,128)S(1)} %get-tuple-element.559, pred[256,512]{0,1:T(8,128)(4,1)S(1)} %broadcast_compare_fusion, ...), kind=kOutput, calls=%fused_computation.10 | convolution fusion | flops 815529984 | bytes 13526016 | tf_op jit(solution)/shard_map/while/body/eval_jaxpr/cond/branch_1_fun/hqk,khd->qhd/dot_general | solution.py:56
  277.8 85.6 %all-gather.14.cloned.1.call-done = bf16[4096,12,128]{0,2,1:T(8,128)(2,1)} async-done(((bf16[256,12,128]{0,2,1:T(8,128)(2,1)}), bf16[4096,12,128]{0,2,1:T(8,128)(2,1)}) %all-gather.14.cloned.1.call-update) | async-done | bytes 12582928 | tf_op jit(solution)/shard_map/all_gather | solution.py:144
  363.4 16.7 %copy.36 = bf16[4096,12,128]{2,0,1:T(8,128)(2,1)} copy(bf16[4096,12,128]{0,2,1:T(8,128)(2,1)} %all-gather.14.cloned.1.call-done) | data formatting | bytes 25165824
  380.1 84.3 %all-gather.12.cloned.1.call-done = bf16[4096,12,128]{2,0,1:T(8,128)(2,1)} async-done(((bf16[256,12,128]{2,0,1:T(8,128)(2,1)}), bf16[4096,12,128]{2,0,1:T(8,128)(2,1)}) %all-gather.12.cloned.1.call-update) | async-done | bytes 12582928 | tf_op jit(solution)/shard_map/all_gather | solution.py:143
  465.9 129.6 %while.38 = (s32[]{:T(128)}, f32[256,12,128]{0,2,1:T(8,128)}, f32[256,12,128]{0,2,1:T(8,128)S(1)}, s32[]{:T(128)}, bf16[4096,12,128]{2,0,1:T(8,128)(2,1)}, /*ind...) while((s32[]{:T(128)}, f32[256,12,128]{0,2,1:T(8,128)}, ...), condition=%wide.region_9.10_spmd.clone, body=%wide.region_6.9_spmd.clone.sunk | while | flops 1627652864 | bytes 58770808 | solution.py:111
  466.6 15.6 %conditional.7 = ((f32[256,12,128]{0,2,1:T(8,128)}, f32[256,12,128]{0,2,1:T(8,128)S(1)})) conditional(s32[]{:T(128)} %convert_element_type.63, (f32[256,12,128]{0,2,1:T(8,128)}, f32[256,12,128]{0,2,1:T(8,128)S(1)}) %tuple.108, (s32[]{:T(128)}, bf16[4096,12,128]{2,0,1:T(8,128)(2,1)}, s32[]{:T(128)}, bf16[256,12,128]{2,0,1:T(8,128)(2,1)S(1)}, ...), branch_computations={%region_7.7_spmd, %region_8.8_spmd} | conditional | flops 1627652864 | bytes 58769512 | solution.py:106
  471.7 3.7 bitcast_add_fusion.1
  475.4 6.7 %bitcast_add_fusion.2 = f32[256,12,128]{0,2,1:T(8,128)} fusion(f32[256,12,128]{0,2,1:T(8,128)} %get-tuple-element.574, f32[12,512,256]{2,1,0:T(8,128)} %copy-done, f32[12,512]{1,0:T(8,128)S(1)} %get-tuple-element.768, f32[12,512]{1,0:T(8,128)S(1)} %get-tuple-element.769, pred[512,256]{1,0:T(8,128)(4,1)S(1)} %broadcast_compare_fusion.1, ...), kind=kOutput, calls=%fused_computation.34 | convolution fusion | flops 815529984 | bytes 13550592 | tf_op jit(solution)/shard_map/while/body/eval_jaxpr/cond/branch_1_fun/hqk,qhd->khd/dot_general | solution.py:96
  482.8 15.6 %conditional.7 = ((f32[256,12,128]{0,2,1:T(8,128)}, f32[256,12,128]{0,2,1:T(8,128)S(1)})) conditional(s32[]{:T(128)} %convert_element_type.63, (f32[256,12,128]{0,2,1:T(8,128)}, f32[256,12,128]{0,2,1:T(8,128)S(1)}) %tuple.108, (s32[]{:T(128)}, bf16[4096,12,128]{2,0,1:T(8,128)(2,1)}, s32[]{:T(128)}, bf16[256,12,128]{2,0,1:T(8,128)(2,1)S(1)}, ...), branch_computations={%region_7.7_spmd, %region_8.8_spmd} | conditional | flops 1627652864 | bytes 58769512 | solution.py:106
  491.6 6.7 %bitcast_add_fusion.2 = f32[256,12,128]{0,2,1:T(8,128)} fusion(f32[256,12,128]{0,2,1:T(8,128)} %get-tuple-element.574, f32[12,512,256]{2,1,0:T(8,128)} %copy-done, f32[12,512]{1,0:T(8,128)S(1)} %get-tuple-element.768, f32[12,512]{1,0:T(8,128)S(1)} %get-tuple-element.769, pred[512,256]{1,0:T(8,128)(4,1)S(1)} %broadcast_compare_fusion.1, ...), kind=kOutput, calls=%fused_computation.34 | convolution fusion | flops 815529984 | bytes 13550592 | tf_op jit(solution)/shard_map/while/body/eval_jaxpr/cond/branch_1_fun/hqk,qhd->khd/dot_general | solution.py:96
  499.0 15.5 %conditional.7 = ((f32[256,12,128]{0,2,1:T(8,128)}, f32[256,12,128]{0,2,1:T(8,128)S(1)})) conditional(s32[]{:T(128)} %convert_element_type.63, (f32[256,12,128]{0,2,1:T(8,128)}, f32[256,12,128]{0,2,1:T(8,128)S(1)}) %tuple.108, (s32[]{:T(128)}, bf16[4096,12,128]{2,0,1:T(8,128)(2,1)}, s32[]{:T(128)}, bf16[256,12,128]{2,0,1:T(8,128)(2,1)S(1)}, ...), branch_computations={%region_7.7_spmd, %region_8.8_spmd} | conditional | flops 1627652864 | bytes 58769512 | solution.py:106
  507.8 6.7 %bitcast_add_fusion.2 = f32[256,12,128]{0,2,1:T(8,128)} fusion(f32[256,12,128]{0,2,1:T(8,128)} %get-tuple-element.574, f32[12,512,256]{2,1,0:T(8,128)} %copy-done, f32[12,512]{1,0:T(8,128)S(1)} %get-tuple-element.768, f32[12,512]{1,0:T(8,128)S(1)} %get-tuple-element.769, pred[512,256]{1,0:T(8,128)(4,1)S(1)} %broadcast_compare_fusion.1, ...), kind=kOutput, calls=%fused_computation.34 | convolution fusion | flops 815529984 | bytes 13550592 | tf_op jit(solution)/shard_map/while/body/eval_jaxpr/cond/branch_1_fun/hqk,qhd->khd/dot_general | solution.py:96
  515.2 15.5 %conditional.7 = ((f32[256,12,128]{0,2,1:T(8,128)}, f32[256,12,128]{0,2,1:T(8,128)S(1)})) conditional(s32[]{:T(128)} %convert_element_type.63, (f32[256,12,128]{0,2,1:T(8,128)}, f32[256,12,128]{0,2,1:T(8,128)S(1)}) %tuple.108, (s32[]{:T(128)}, bf16[4096,12,128]{2,0,1:T(8,128)(2,1)}, s32[]{:T(128)}, bf16[256,12,128]{2,0,1:T(8,128)(2,1)S(1)}, ...), branch_computations={%region_7.7_spmd, %region_8.8_spmd} | conditional | flops 1627652864 | bytes 58769512 | solution.py:106
  524.0 6.7 %bitcast_add_fusion.2 = f32[256,12,128]{0,2,1:T(8,128)} fusion(f32[256,12,128]{0,2,1:T(8,128)} %get-tuple-element.574, f32[12,512,256]{2,1,0:T(8,128)} %copy-done, f32[12,512]{1,0:T(8,128)S(1)} %get-tuple-element.768, f32[12,512]{1,0:T(8,128)S(1)} %get-tuple-element.769, pred[512,256]{1,0:T(8,128)(4,1)S(1)} %broadcast_compare_fusion.1, ...), kind=kOutput, calls=%fused_computation.34 | convolution fusion | flops 815529984 | bytes 13550592 | tf_op jit(solution)/shard_map/while/body/eval_jaxpr/cond/branch_1_fun/hqk,qhd->khd/dot_general | solution.py:96
  531.3 15.5 %conditional.7 = ((f32[256,12,128]{0,2,1:T(8,128)}, f32[256,12,128]{0,2,1:T(8,128)S(1)})) conditional(s32[]{:T(128)} %convert_element_type.63, (f32[256,12,128]{0,2,1:T(8,128)}, f32[256,12,128]{0,2,1:T(8,128)S(1)}) %tuple.108, (s32[]{:T(128)}, bf16[4096,12,128]{2,0,1:T(8,128)(2,1)}, s32[]{:T(128)}, bf16[256,12,128]{2,0,1:T(8,128)(2,1)S(1)}, ...), branch_computations={%region_7.7_spmd, %region_8.8_spmd} | conditional | flops 1627652864 | bytes 58769512 | solution.py:106
  536.5 3.7 bitcast_add_fusion.1
  540.2 6.7 %bitcast_add_fusion.2 = f32[256,12,128]{0,2,1:T(8,128)} fusion(f32[256,12,128]{0,2,1:T(8,128)} %get-tuple-element.574, f32[12,512,256]{2,1,0:T(8,128)} %copy-done, f32[12,512]{1,0:T(8,128)S(1)} %get-tuple-element.768, f32[12,512]{1,0:T(8,128)S(1)} %get-tuple-element.769, pred[512,256]{1,0:T(8,128)(4,1)S(1)} %broadcast_compare_fusion.1, ...), kind=kOutput, calls=%fused_computation.34 | convolution fusion | flops 815529984 | bytes 13550592 | tf_op jit(solution)/shard_map/while/body/eval_jaxpr/cond/branch_1_fun/hqk,qhd->khd/dot_general | solution.py:96
  547.5 15.5 %conditional.7 = ((f32[256,12,128]{0,2,1:T(8,128)}, f32[256,12,128]{0,2,1:T(8,128)S(1)})) conditional(s32[]{:T(128)} %convert_element_type.63, (f32[256,12,128]{0,2,1:T(8,128)}, f32[256,12,128]{0,2,1:T(8,128)S(1)}) %tuple.108, (s32[]{:T(128)}, bf16[4096,12,128]{2,0,1:T(8,128)(2,1)}, s32[]{:T(128)}, bf16[256,12,128]{2,0,1:T(8,128)(2,1)S(1)}, ...), branch_computations={%region_7.7_spmd, %region_8.8_spmd} | conditional | flops 1627652864 | bytes 58769512 | solution.py:106
  556.4 6.7 %bitcast_add_fusion.2 = f32[256,12,128]{0,2,1:T(8,128)} fusion(f32[256,12,128]{0,2,1:T(8,128)} %get-tuple-element.574, f32[12,512,256]{2,1,0:T(8,128)} %copy-done, f32[12,512]{1,0:T(8,128)S(1)} %get-tuple-element.768, f32[12,512]{1,0:T(8,128)S(1)} %get-tuple-element.769, pred[512,256]{1,0:T(8,128)(4,1)S(1)} %broadcast_compare_fusion.1, ...), kind=kOutput, calls=%fused_computation.34 | convolution fusion | flops 815529984 | bytes 13550592 | tf_op jit(solution)/shard_map/while/body/eval_jaxpr/cond/branch_1_fun/hqk,qhd->khd/dot_general | solution.py:96
  563.7 15.5 %conditional.7 = ((f32[256,12,128]{0,2,1:T(8,128)}, f32[256,12,128]{0,2,1:T(8,128)S(1)})) conditional(s32[]{:T(128)} %convert_element_type.63, (f32[256,12,128]{0,2,1:T(8,128)}, f32[256,12,128]{0,2,1:T(8,128)S(1)}) %tuple.108, (s32[]{:T(128)}, bf16[4096,12,128]{2,0,1:T(8,128)(2,1)}, s32[]{:T(128)}, bf16[256,12,128]{2,0,1:T(8,128)(2,1)S(1)}, ...), branch_computations={%region_7.7_spmd, %region_8.8_spmd} | conditional | flops 1627652864 | bytes 58769512 | solution.py:106
  572.6 6.7 %bitcast_add_fusion.2 = f32[256,12,128]{0,2,1:T(8,128)} fusion(f32[256,12,128]{0,2,1:T(8,128)} %get-tuple-element.574, f32[12,512,256]{2,1,0:T(8,128)} %copy-done, f32[12,512]{1,0:T(8,128)S(1)} %get-tuple-element.768, f32[12,512]{1,0:T(8,128)S(1)} %get-tuple-element.769, pred[512,256]{1,0:T(8,128)(4,1)S(1)} %broadcast_compare_fusion.1, ...), kind=kOutput, calls=%fused_computation.34 | convolution fusion | flops 815529984 | bytes 13550592 | tf_op jit(solution)/shard_map/while/body/eval_jaxpr/cond/branch_1_fun/hqk,qhd->khd/dot_general | solution.py:96
  579.9 15.5 %conditional.7 = ((f32[256,12,128]{0,2,1:T(8,128)}, f32[256,12,128]{0,2,1:T(8,128)S(1)})) conditional(s32[]{:T(128)} %convert_element_type.63, (f32[256,12,128]{0,2,1:T(8,128)}, f32[256,12,128]{0,2,1:T(8,128)S(1)}) %tuple.108, (s32[]{:T(128)}, bf16[4096,12,128]{2,0,1:T(8,128)(2,1)}, s32[]{:T(128)}, bf16[256,12,128]{2,0,1:T(8,128)(2,1)S(1)}, ...), branch_computations={%region_7.7_spmd, %region_8.8_spmd} | conditional | flops 1627652864 | bytes 58769512 | solution.py:106
  588.8 6.7 %bitcast_add_fusion.2 = f32[256,12,128]{0,2,1:T(8,128)} fusion(f32[256,12,128]{0,2,1:T(8,128)} %get-tuple-element.574, f32[12,512,256]{2,1,0:T(8,128)} %copy-done, f32[12,512]{1,0:T(8,128)S(1)} %get-tuple-element.768, f32[12,512]{1,0:T(8,128)S(1)} %get-tuple-element.769, pred[512,256]{1,0:T(8,128)(4,1)S(1)} %broadcast_compare_fusion.1, ...), kind=kOutput, calls=%fused_computation.34 | convolution fusion | flops 815529984 | bytes 13550592 | tf_op jit(solution)/shard_map/while/body/eval_jaxpr/cond/branch_1_fun/hqk,qhd->khd/dot_general | solution.py:96
  (118 shorter events, 79.4 us)
Async XLA Ops:
  7.2 44.1 %all-gather.10.cloned.1.call-start = ((), (), s32[]{:S(2)}) async-start(), calls=%async_computation.2 | async-start | bytes 3932160 | tf_op jit(solution)/shard_map/all_gather | solution.py:123
  7.9 149.0 %all-gather.6.cloned.1.call-start = ((), (), s32[]{:S(2)}) async-start(), calls=%async_computation | async-start | bytes 13369344 | tf_op jit(solution)/shard_map/all_gather | solution.py:135
  8.6 250.0 %all-gather.8.cloned.1.call-start = ((), (), s32[]{:S(2)}) async-start(), calls=%async_computation.1 | async-start | bytes 13369344 | tf_op jit(solution)/shard_map/all_gather | solution.py:136
  9.4 55.6 %copy-start.4 = (f32[256,12]{0,1:T(8,128)S(1)}, f32[256,12]{0,1:T(8,128)}, u32[]{:S(2)}) copy-start(f32[256,12]{0,1:T(8,128)} %param.21) | copy-start | bytes 36868
  9.4 354.0 %all-gather.14.cloned.1.call-start = ((), (), s32[]{:S(2)}) async-start(), calls=%async_computation.4 | async-start | bytes 13369344 | tf_op jit(solution)/shard_map/all_gather | solution.py:144
  61.8 197.0 %copy-start.1 = (bf16[256,12,128]{2,0,1:T(8,128)(2,1)S(1)}, bf16[256,12,128]{2,0,1:T(8,128)(2,1)}, u32[]{:S(2)}) copy-start(bf16[256,12,128]{2,0,1:T(8,128)(2,1)} %param.15) | copy-start | bytes 2359300
  63.0 401.4 %all-gather.12.cloned.1.call-start = ((), (), s32[]{:S(2)}) async-start(), calls=%async_computation.3 | async-start | bytes 13369344 | tf_op jit(solution)/shard_map/all_gather | solution.py:143
  277.8 188.1 %copy-start.2 = (bf16[256,12,128]{2,0,1:T(8,128)(2,1)S(1)}, bf16[256,12,128]{2,0,1:T(8,128)(2,1)}, u32[]{:S(2)}) copy-start(bf16[256,12,128]{2,0,1:T(8,128)(2,1)} %param.16) | copy-start | bytes 2359300
  277.8 188.1 %copy-start.3 = (bf16[256,12,128]{2,0,1:T(8,128)(2,1)S(1)}, bf16[256,12,128]{2,0,1:T(8,128)(2,1)}, u32[]{:S(2)}) copy-start(bf16[256,12,128]{2,0,1:T(8,128)(2,1)} %param.17) | copy-start | bytes 2359300
  469.0 2.7 copy-start
  485.2 2.7 copy-start
  501.4 2.7 copy-start
  517.6 2.7 copy-start
  533.8 2.7 copy-start
  550.0 2.7 copy-start
  566.2 2.7 copy-start
  582.3 2.7 copy-start
Sparse Core Ops, SparseCore 0:
  9.5 41.7 all-gather.9
  53.5 103.4 all-gather.5
  159.1 99.4 all-gather.7
  261.2 102.1 all-gather.13
  365.4 98.9 all-gather.11
where the time goes:
time: 608 us; the launch traced here: 606 us
  waiting for transfers between devices  358 us (59%)
  matrix products  125 us (21%)
  local copies, waits for them, and re-layouts  47.5 us (8%)
  blocking collectives  45.6 us (8%)
  between operations  13.9 us (2%)
  loops' own time  11.2 us (2%)
    all_gather x1, waiting for transfers between devices, body(): lax.all_gather(value_vectors, 'ctx', axis=0, tiled=True)  102 us
    all_gather x1, waiting for transfers between devices, body(): lax.all_gather(attn_grad, 'ctx', axis=0, tiled=True)  85.6 us
    all_gather x1, waiting for transfers between devices, body(): lax.all_gather(queries, 'ctx', axis=0, tiled=True)  84.3 us
    dot_general x8, matrix products, key_update(): jnp.einsum('hqk,qhd->khd', score_grad, query_block, preferred_element_typ...  53.6 us
    all_gather x1, waiting for transfers between devices, body(): lax.all_gather(key_vectors, 'ctx', axis=0, tiled=True)  41.9 us
    all_gather x1, waiting for transfers between devices, body(): lax.all_gather(output_grad, 'head', axis=1, tiled=True)  41.9 us
    dot_general x8, matrix products, key_update(): jnp.einsum('hqk,qhd->khd', prob_low, grad_block, preferred_element_type=j...  29.7 us
    all_gather x1, blocking collectives, body(): lax.all_gather(own_total, 'ctx', axis=1, tiled=True)  24.9 us
  transfers between devices with their start and end apart: 5, of which 5 were waited for; matrix products, arithmetic and copies ran while one was open for 8% of the time, Pallas kernels for 0%

commit v1 on v0

v1 whole, which is shorter than its diff:
```python
import functools
import math

import jax
import jax.numpy as jnp
from jax import lax
from jax.experimental import pallas as pl
from jax.experimental.pallas import tpu as pltpu
from jax.sharding import PartitionSpec as P

F32 = jnp.float32
BF16 = jnp.bfloat16
LANES = 128
NT = (((1,), (1,)), ((), ()))
NN = (((1,), (0,)), ((), ()))


def stat_rows(rows):
    return -(-6 * (rows // LANES) // 16) * 16


def dot(a, b, dims):
    return lax.dot_general(a, b, dims, preferred_element_type=F32)


def pack_kernel(meta_ref, grad_ref, out_ref, total_ref, packed_ref, *, heads):
    rows, _ = grad_ref.shape
    halves = rows // LANES
    head = meta_ref[pl.program_id(0)] * heads + pl.program_id(1)
    grad = grad_ref[...]
    product = grad.astype(F32) * out_ref[...].astype(F32)
    delta = jnp.sum(jnp.transpose(product), axis=0, keepdims=True)
    total = total_ref[pl.ds(head, 1), :]
    pieces = []
    rest = [total, delta]
    for _ in range(3):
        high = [part.astype(BF16).astype(F32) for part in rest]
        rest = [part - top for part, top in zip(rest, high)]
        for top in high:
            pieces += [top[:, i * LANES : (i + 1) * LANES] for i in range(halves)]
    spare = stat_rows(rows) - len(pieces)
    if spare:
        pieces.append(jnp.zeros((spare, LANES), F32))
    packed_ref[0:rows, :] = grad
    packed_ref[rows:, :] = jnp.concatenate(pieces, axis=0).astype(BF16)


def pack_grads(members, grad_flat, out_heads, totals, heads):
    all_heads, rows, width = out_heads.shape
    group = all_heads // heads
    extra = stat_rows(rows)
    return pl.pallas_call(
        functools.partial(pack_kernel, heads=heads),
        grid_spec=pltpu.PrefetchScalarGridSpec(
            num_scalar_prefetch=1,
            grid=(group, heads),
            in_specs=[
                pl.BlockSpec((rows, width), lambda d, h, m: (0, m[d] * heads + h)),
                pl.BlockSpec((None, rows, width), lambda d, h, m: (m[d] * heads + h, 0, 0)),
                pl.BlockSpec((all_heads, rows), lambda d, h, m: (0, 0)),
            ],
            out_specs=pl.BlockSpec((None, None, rows + extra, width), lambda d, h, m: (d, h, 0, 0)),
        ),
        out_shape=jax.ShapeDtypeStruct((group, heads, rows + extra, width), BF16),
        name="pack_grads",
    )(members, grad_flat, out_heads, totals)


def read_stats(block, rows):
    halves = rows // LANES
    values = block.astype(F32)
    span = 2 * halves
    whole = values[0:span] + values[span : 2 * span] + values[2 * span : 3 * span]
    total = jnp.concatenate([whole[i : i + 1] for i in range(halves)], axis=1)
    delta = jnp.concatenate([whole[halves + i : halves + i + 1] for i in range(halves)], axis=1)
    return total, delta


def column(row):
    return jnp.transpose(jnp.broadcast_to(row, (LANES, row.shape[1])))[:, 0:1]


def positions(meta_ref, first, count, rows, shape, axis):
    place = lax.broadcasted_iota(jnp.int32, shape, axis)
    where = place + (meta_ref[1 + first] * rows)
    for i in range(1, count):
        where = jnp.where(place >= i * rows, place + (meta_ref[1 + first + i] - i) * rows, where)
    return where


def key_kernel(
    meta_ref, query_ref, grad_ref, key_ref, value_ref, *rest, diagonal, last, factor, tile
):
    if diagonal:
        dk_out, dv_out = rest
    else:
        dk_in, dv_in, dk_out, dv_out = rest
    group, rows, width = query_ref.shape
    first = pl.program_id(1) * tile

    def compute():
        keys = key_ref[...].reshape(tile * rows, width)
        values = value_ref[...].reshape(tile * rows, width)
        dk = jnp.zeros((tile * rows, width), F32)
        dv = jnp.zeros((tile * rows, width), F32)
        for g in range(group):
            queries = query_ref[g]
            grads = grad_ref[g, 0:rows, :]
            total, delta = read_stats(grad_ref[g, rows:, :], rows)
            scores = dot(keys, queries, NT) * factor
            if diagonal:
                key_pos = positions(meta_ref, first, tile, rows, scores.shape, 0)
                query_pos = positions(meta_ref, g, 1, rows, scores.shape, 1)
                scores = jnp.where(key_pos <= query_pos, scores, -jnp.inf)
            prob = jnp.exp(scores - total)
            dv = dv + dot(prob.astype(BF16), grads, NN)
            prob_grad = dot(values, grads, NT)
            score_grad = (prob * (prob_grad - delta)).astype(BF16)
            dk = dk + dot(score_grad, queries, NN)
        return dk, dv

    def emit(dk, dv):
        if not diagonal:
            dk = dk + dk_in[...].reshape(dk.shape)
            dv = dv + dv_in[...].reshape(dv.shape)
        if last:
            dk = dk * factor
        dk_out[...] = dk.reshape(dk_out.shape).astype(dk_out.dtype)
        dv_out[...] = dv.reshape(dv_out.shape).astype(dv_out.dtype)

    if diagonal:
        emit(*compute())
    else:
        pl.when(meta_ref[0] > 0)(lambda: emit(*compute()))

        @pl.when(meta_ref[0] == 0)
        def _():
            emit(jnp.zeros((tile * rows, width), F32), jnp.zeros((tile * rows, width), F32))


def query_kernel(
    meta_ref, query_ref, grad_ref, key_ref, value_ref, *rest, diagonal, last, factor, tile
):
    if diagonal:
        (dq_out,) = rest
    else:
        dq_in, dq_out = rest
    group, rows, width = key_ref.shape
    first = pl.program_id(1) * tile

    def compute():
        queries = query_ref[...].reshape(tile * rows, width)
        grads = jnp.concatenate([grad_ref[i, 0:rows, :] for i in range(tile)], axis=0)
        stats = [read_stats(grad_ref[i, rows:, :], rows) for i in range(tile)]
        total = jnp.concatenate([column(part[0]) for part in stats], axis=0)
        delta = jnp.concatenate([column(part[1]) for part in stats], axis=0)
        dq = jnp.zeros((tile * rows, width), F32)
        for g in range(group):
            keys = key_ref[g]
            scores = dot(queries, keys, NT) * factor
            if diagonal:
                query_pos = positions(meta_ref, first, tile, rows, scores.shape, 0)
                key_pos = positions(meta_ref, g, 1, rows, scores.shape, 1)
                scores = jnp.where(key_pos <= query_pos, scores, -jnp.inf)
            prob = jnp.exp(scores - total)
            prob_grad = dot(grads, value_ref[g], NT)
            score_grad = (prob * (prob_grad - delta)).astype(BF16)
            dq = dq + dot(score_grad, keys, NN)
        return dq

    def emit(dq):
        if not diagonal:
            dq = dq + dq_in[...].reshape(dq.shape)
        if last:
            dq = dq * factor
        dq_out[...] = dq.reshape(dq_out.shape).astype(dq_out.dtype)

    if diagonal:
        emit(compute())
    else:
        pl.when(meta_ref[0] > 0)(lambda: emit(compute()))

        @pl.when(meta_ref[0] == 0)
        def _():
            emit(jnp.zeros((tile * rows, width), F32))


def call_pass(kernel, meta, queries, grads, keys, values, running, *, diagonal, last, factor):
    group, heads, rows, width = queries.shape
    packed = grads.shape[2]
    tile = 2 if group % 2 == 0 else 1
    by_key = kernel is key_kernel

    def whole(height):
        return pl.BlockSpec((group, None, height, width), lambda h, t, m: (0, h, 0, 0))

    def part(height):
        return pl.BlockSpec((tile, None, height, width), lambda h, t, m: (t, h, 0, 0))

    query_side, key_side = (whole, part) if by_key else (part, whole)
    outputs = 2 if by_key else 1
    out_type = BF16 if last else F32
    pairs = heads * (group * rows) ** 2
    products = 4 if by_key else 3
    return pl.pallas_call(
        functools.partial(kernel, diagonal=diagonal, last=last, factor=factor, tile=tile),
        grid_spec=pltpu.PrefetchScalarGridSpec(
            num_scalar_prefetch=1,
            grid=(heads, group // tile),
            in_specs=[query_side(rows), query_side(packed), key_side(rows), key_side(rows)]
            + [part(rows)] * len(running),
            out_specs=[part(rows)] * outputs,
        ),
        out_shape=[jax.ShapeDtypeStruct(queries.shape, out_type)] * outputs,
        compiler_params=pltpu.CompilerParams(vmem_limit_bytes=48 * 1024 * 1024),
        cost_estimate=pl.CostEstimate(
            flops=2 * products * pairs * width,
            bytes_accessed=8 * queries.size * 2,
            transcendentals=pairs,
        ),
        name="key_pass" if by_key else "query_pass",
    )(meta, queries, grads, keys, values, *running)


def body(queries, key_vectors, value_vectors, attn_output, output_grad, w_out, log_total):
    rows, head_count, width = queries.shape
    factor = width ** (-0.5)
    ctx_count = lax.axis_size("ctx")
    head_size = lax.axis_size("head")
    ctx_index = lax.axis_index("ctx")
    group = math.gcd(ctx_count, head_count)
    group = group & -group
    heads = head_count // group
    blocks = ctx_count // group
    block_index = ctx_index // group
    member = ctx_index % group
    members = jnp.bitwise_xor(member, jnp.arange(group, dtype=jnp.int32))

    def swap(d):
        return [(i, (i // group) * group + (i % group ^ d)) for i in range(ctx_count)]

    def spread(array, axis):
        own = [lax.index_in_dim(array, 0, axis, keepdims=False)]
        for d in range(1, group):
            own.append(lax.ppermute(lax.index_in_dim(array, d, axis, keepdims=False), "ctx", swap(d)))
        return jnp.stack(own, axis=axis)

    def by_member(array):
        grouped = jnp.transpose(array, (1, 0, 2)).reshape(group, heads, rows, width)
        return jnp.stack([lax.dynamic_index_in_dim(grouped, members[d], 0, False) for d in range(group)])

    if head_size == 2:
        other = lax.ppermute(output_grad, "head", [(0, 1), (1, 0)])
        lower = lax.axis_index("head") == 0
        features = jnp.concatenate(
            [jnp.where(lower, output_grad, other), jnp.where(lower, other, output_grad)], axis=1
        )
    else:
        features = lax.all_gather(output_grad, "head", axis=1, tiled=True)

    key_value = spread(jnp.stack([by_member(key_vectors), by_member(value_vectors)]), 1)
    own_keys, own_values = key_value[0], key_value[1]
    own_queries = spread(by_member(queries), 0)

    grad_flat = lax.dot_general(features, w_out, NT, preferred_element_type=F32).astype(BF16)
    packed = pack_grads(
        members,
        grad_flat,
        jnp.transpose(attn_output, (1, 0, 2)),
        jnp.transpose(log_total, (1, 0)),
        heads,
    )
    own_grads = spread(packed, 0)

    def meta_of(valid):
        return jnp.concatenate([jnp.asarray(valid, jnp.int32).reshape(1), members])

    always = meta_of(1)
    common = dict(factor=factor)
    only = blocks == 1
    (dq,) = call_pass(
        query_kernel, always, own_queries, own_grads, own_keys, own_values, [],
        diagonal=True, last=only, **common,
    )
    dk, dv = call_pass(
        key_kernel, always, own_queries, own_grads, own_keys, own_values, [],
        diagonal=True, last=only, **common,
    )
    up = [own_keys, own_values]
    down = [own_queries, own_grads]
    for step in range(1, blocks):
        forward = [
            (z * group + i, (z + 1) * group + i) for z in range(step - 1, blocks - 1) for i in range(group)
        ]
        backward = [
            (z * group + i, (z - 1) * group + i) for z in range(1, blocks - step + 1) for i in range(group)
        ]
        up = [lax.ppermute(array, "ctx", forward) for array in up]
        down = [lax.ppermute(array, "ctx", backward) for array in down]
        last = step == blocks - 1
        (dq,) = call_pass(
            query_kernel, meta_of(block_index >= step), own_queries, own_grads, *up, [dq],
            diagonal=False, last=last, **common,
        )
        dk, dv = call_pass(
            key_kernel, meta_of(block_index < blocks - step), *down, own_keys, own_values, [dk, dv],
            diagonal=False, last=last, **common,
        )

    def collect(array):
        pieces = spread(array, 0)
        ordered = jnp.stack([lax.dynamic_index_in_dim(pieces, member ^ g, 0, False) for g in range(group)])
        return jnp.transpose(ordered.reshape(head_count, rows, width), (1, 0, 2))

    return collect(dq), collect(dk), collect(dv)


def solution(mesh):
    in_specs = (
        P("ctx", "head", None),
        P("ctx", "head", None),
        P("ctx", "head", None),
        P("ctx", "head", None),
        P("ctx", "head"),
        P("head", None),
        P("ctx", "head"),
    )
    out_specs = (P("ctx", "head", None), P("ctx", "head", None), P("ctx", "head", None))
    return jax.shard_map(body, mesh=mesh, in_specs=in_specs, out_specs=out_specs, check_vma=False)
```

time: 608 us -> 226 us (0.37)
  waiting for transfers between devices: 358 us -> 77.2 us
  matrix products: 125 us -> 11.4 us
  Pallas kernels: 0 us -> 72.4 us
  blocking collectives: 45.6 us -> 0 us
  local copies, waits for them, and re-layouts: 47.5 us -> 9.57 us
  starting transfers between devices: 0.19 us -> 36.6 us
  loops' own time: 11.2 us -> 0 us
    all_gather x5 -> x0, waiting for transfers between devices: 355 us -> none  [the longest x1 102 us: body(): lax.all_gather(value_vectors, 'ctx', axis=0, tiled=True)]
    dot_general x27 -> x1, matrix products: 125 us -> 11.4 us  [body(): lax.dot_general(features, w_out, NT, preferred_element_type=F32)]
    ppermute x0 -> x31, waiting for transfers between devices: none -> 77.2 us  [the longest x18 43 us: spread(): lax.ppermute(lax.index_in_dim(array, d, axis, keepdims=False), 'ctx', swa...]
    pallas_call x0 -> x9, Pallas kernels: none -> 72.4 us  [the longest x8 64.1 us: call_pass(): pl.pallas_call(functools.partial(kernel, diagonal=diagonal, last=last, fa...]
    all_gather x2 -> x0, blocking collectives: 45.6 us -> none  [the longest x1 24.9 us: body(): lax.all_gather(own_total, 'ctx', axis=1, tiled=True)]
    ppermute x0 -> x31, starting transfers between devices: none -> 36.6 us  [the longest x18 13.1 us: spread(): lax.ppermute(lax.index_in_dim(array, d, axis, keepdims=False), 'ctx', swa...]
    unnamed x11 -> x22, local copies, waits for them, and re-layouts: 19.7 us -> 5.05 us
    cond x16 -> x0, local copies, waits for them, and re-layouts: 13.4 us -> none
  transfers between devices with their start and end apart: 5 -> 31, of which waited for: 5 -> 16; matrix products, arithmetic and copies ran while one was open for 8% -> 10% of each run, Pallas kernels for 0% -> 27%
where the time goes in v1:
time: 226 us; the launch traced here: 225 us
  waiting for transfers between devices  77.2 us (34%)
  Pallas kernels  72.4 us (32%)
  starting transfers between devices  36.6 us (16%)
  matrix products  11.4 us (5%)
  local copies, waits for them, and re-layouts  9.57 us (4%)
  other arithmetic  9.13 us (4%)
  between operations  8.47 us (4%)
    pallas_call x8, Pallas kernels, call_pass(): pl.pallas_call(functools.partial(kernel, diagonal=diagonal, last=last, fa...  64.1 us
    ppermute x18, waiting for transfers between devices, spread(): lax.ppermute(lax.index_in_dim(array, d, axis, keepdims=False), 'ctx', swa...  43 us
    ppermute x6, waiting for transfers between devices, body(): down = [lax.ppermute(array, 'ctx', backward) for array in down]  30.3 us
    ppermute x18, starting transfers between devices, spread(): lax.ppermute(lax.index_in_dim(array, d, axis, keepdims=False), 'ctx', swa...  13.1 us
    ppermute x6, starting transfers between devices, body(): up = [lax.ppermute(array, 'ctx', forward) for array in up]  12.6 us
    dot_general x1, matrix products, body(): lax.dot_general(features, w_out, NT, preferred_element_type=F32)  11.4 us
    pallas_call x1, Pallas kernels, pack_grads(): pl.pallas_call(functools.partial(pack_kernel, heads=heads), grid_spec=plt...  8.27 us
    ppermute x6, starting transfers between devices, body(): down = [lax.ppermute(array, 'ctx', backward) for array in down]  7.89 us
  transfers between devices with their start and end apart: 31, of which 16 were waited for; matrix products, arithmetic and copies ran while one was open for 10% of the time, Pallas kernels for 27%

profile of v1, /device:TPU:0, one launch (start us, length us, event | category | flops | bytes accessed | tf_op | source)
XLA Modules:
  0.0 224.7 jit_solution(5769021544003347513)
XLA Ops:
  0.7 3.0 %collective-permute-start.3 = (bf16[256,2560]{1,0:T(8,128)(2,1)}, bf16[256,2560]{1,0:T(8,128)(2,1)}, u32[]{:S(2)}, u32[]{:S(2)}) collective-permute-start(bf16[256,2560]{1,0:T(8,128)(2,1)} %param.11), channel_id=1, source_target_pairs={{0,1},{1,0},{2,3},{3,2},{4,5},{5,4},{6,7},{7,6},{8,9},{9,8},{10,11... | collective-permute-start | bytes 3932168 | tf_op jit(solution)/shard_map/ppermute | solution.py:253
  11.7 2.0 constant_dynamic-slice_fusion.20
  17.9 3.6 %collective-permute-done.1 = bf16[3,256,128]{2,1,0:T(8,128)(2,1)S(1)} collective-permute-done((bf16[3,256,128]{2,1,0:T(8,128)(2,1)S(1)}, bf16[3,256,128]{2,1,0:T(8,128)(2,1)S(1)}, u32[]{:S(2)}, u32[]{:S(2)}) %collective-permute-start.1) | collective-permute-done | bytes 196640 | tf_op jit(solution)/shard_map/ppermute | solution.py:245
  21.5 3.2 %collective-permute-done.2 = bf16[3,256,128]{2,1,0:T(8,128)(2,1)} collective-permute-done((bf16[3,256,128]{2,1,0:T(8,128)(2,1)S(1)}, bf16[3,256,128]{2,1,0:T(8,128)(2,1)}, u32[]{:S(2)}, u32[]{:S(2)}) %collective-permute-start.2) | collective-permute-done | bytes 196640 | tf_op jit(solution)/shard_map/ppermute | solution.py:245
  30.3 3.8 %collective-permute-done.8 = bf16[2,3,256,128]{3,2,1,0:T(8,128)(2,1)S(1)} collective-permute-done((bf16[2,3,256,128]{3,2,1,0:T(8,128)(2,1)S(1)}, bf16[2,3,256,128]{3,2,1,0:T(8,128)(2,1)S(1)}, u32[]{:S(2)}, u32[]{:S(2)}) %collective-permute-start.8) | collective-permute-done | bytes 393248 | tf_op jit(solution)/shard_map/ppermute | solution.py:245
  34.2 6.0 %collective-permute-done.9 = bf16[2,3,256,128]{3,2,1,0:T(8,128)(2,1)} collective-permute-done((bf16[2,3,256,128]{3,2,1,0:T(8,128)(2,1)S(1)}, bf16[2,3,256,128]{3,2,1,0:T(8,128)(2,1)}, u32[]{:S(2)}, u32[]{:S(2)}) %collective-permute-start.9) | collective-permute-done | bytes 393248 | tf_op jit(solution)/shard_map/ppermute | solution.py:245
  41.5 4.5 %collective-permute-start.10 = (bf16[4,3,256,128]{3,2,1,0:T(8,128)(2,1)S(1)}, bf16[4,3,256,128]{3,2,1,0:T(8,128)(2,1)}, u32[]{:S(2)}, u32[]{:S(2)}) collective-permute-start(bf16[4,3,256,128]{3,2,1,0:T(8,128)(2,1)S(1)} %get-tuple-element.22.key_ref), channel_id=1, source_target_pairs={{0,8},{2,10},{4,12},{6,14},{8,16},{10,18},{12,20},{14,22},{16,24},... | collective-permute-start | bytes 2359304 | tf_op jit(solution)/shard_map/ppermute | solution.py:298
  46.0 3.6 %collective-permute-start.13 = (bf16[4,3,256,128]{3,2,1,0:T(8,128)(2,1)S(1)}, bf16[4,3,256,128]{3,2,1,0:T(8,128)(2,1)}, u32[]{:S(2)}, u32[]{:S(2)}) collective-permute-start(bf16[4,3,256,128]{3,2,1,0:T(8,128)(2,1)S(1)} %get-tuple-element.21.value_ref), channel_id=1, source_target_pairs={{0,8},{2,10},{4,12},{6,14},{8,16},{10,18},{12,20},{14,22},{16,24},... | collective-permute-start | bytes 2359304 | tf_op jit(solution)/shard_map/ppermute | solution.py:298
  49.6 3.0 %broadcast_select_fusion.1 = (bf16[256,2560]{1,0:T(8,128)(2,1)}, bf16[256,2560]{1,0:T(8,128)(2,1)}) fusion(bf16[256,2560]{1,0:T(8,128)(2,1)S(1)} %copy-done.5, bf16[256,2560]{1,0:T(8,128)(2,1)} %collective-permute-done.3, pred[]{:T(512)S(6)} %eq.5), kind=kLoop, calls=%fused_computation.13 | loop fusion | flops 1310720 | bytes 5242881 | tf_op jit(solution)/shard_map/jit(_where)/select_n | solution.py:256
  52.5 11.4 %fusion.4.grad_ref = bf16[256,1536]{1,0:T(8,128)(2,1)} fusion(bf16[1536,5120]{1,0:T(8,128)(2,1)} %param.12, bf16[256,2560]{1,0:T(8,128)(2,1)} %get-tuple-element.20, bf16[256,2560]{1,0:T(8,128)(2,1)} %get-tuple-element.19), kind=kOutput, calls=%fused_computation.4 | convolution fusion | flops 4032167936 | bytes 19136512 | tf_op jit(solution)/shard_map/dot_general | solution.py:265
  63.9 8.3 %pack_grads.1 = bf16[4,3,272,128]{3,2,1,0:T(8,128)(2,1)} custom-call(s32[4]{0:T(128)} %copy-done.9, bf16[256,1536]{1,0:T(8,128)(2,1)} %fusion.4.grad_ref, bf16[12,256,128]{2,1,0:T(8,128)(2,1)} %bitcast.105, f32[12,256]{1,0:T(8,128)} %bitcast.122), custom_call_target="tpu_custom_call" | custom-call | tf_op jit(solution)/shard_map/pack_grads/pallas_call | solution.py:52
  74.2 1.6 collective-permute-start.11
  75.8 3.8 %collective-permute-done.13.value_ref = bf16[4,3,256,128]{3,2,1,0:T(8,128)(2,1)} collective-permute-done((bf16[4,3,256,128]{3,2,1,0:T(8,128)(2,1)S(1)}, bf16[4,3,256,128]{3,2,1,0:T(8,128)(2,1)}, u32[]{:S(2)}, u32[]{:S(2)}) %collective-permute-start.13) | collective-permute-done | bytes 786464 | tf_op jit(solution)/shard_map/ppermute | solution.py:298
  79.6 1.5 collective-permute-start.14
  82.9 6.3 %collective-permute-done.5 = bf16[3,272,128]{2,1,0:T(8,128)(2,1)S(1)} collective-permute-done((bf16[3,272,128]{2,1,0:T(8,128)(2,1)S(1)}, bf16[3,272,128]{2,1,0:T(8,128)(2,1)S(1)}, u32[]{:S(2)}, u32[]{:S(2)}) %collective-permute-start.5) | collective-permute-done | bytes 208928 | tf_op jit(solution)/shard_map/ppermute | solution.py:245
  89.2 3.3 %collective-permute-done.6 = bf16[3,272,128]{2,1,0:T(8,128)(2,1)S(1)} collective-permute-done((bf16[3,272,128]{2,1,0:T(8,128)(2,1)S(1)}, bf16[3,272,128]{2,1,0:T(8,128)(2,1)S(1)}, u32[]{:S(2)}, u32[]{:S(2)}) %collective-permute-start.6) | collective-permute-done | bytes 208928 | tf_op jit(solution)/shard_map/ppermute | solution.py:245
  96.8 8.7 %query_pass.4.rest_0_ = f32[4,3,256,128]{3,2,1,0:T(8,128)S(1)} custom-call(s32[5]{0:T(128)S(1)} %get-tuple-element.70.meta_ref, bf16[4,3,256,128]{3,2,1,0:T(8,128)(2,1)S(1)} %pad_maximum_fusion.2.query_ref, bf16[4,3,272,128]{3,2,1,0:T(8,128)(2,1)S(1)} %pad_maximum_fusion.1.grad_ref, bf16[4,3,256,128]{3,2,1,0:T(8,128)(2,1)S(1)} %get-tuple-element.22.key_ref, ...), custom_call_target="tpu_custom_call" | custom-call | flops 2415919104 | bytes 6291456 | tf_op jit(solution)/shard_map/query_pass/pallas_call | solution.py:205
  105.6 10.1 %key_pass.4 = (f32[4,3,256,128]{3,2,1,0:T(8,128)S(1)}, f32[4,3,256,128]{3,2,1,0:T(8,128)}) custom-call(s32[5]{0:T(128)S(1)} %get-tuple-element.70.meta_ref, bf16[4,3,256,128]{3,2,1,0:T(8,128)(2,1)S(1)} %pad_maximum_fusion.2.query_ref, bf16[4,3,272,128]{3,2,1,0:T(8,128)(2,1)S(1)} %pad_maximum_fusion.1.grad_ref, ...), custom_call_target="tpu_custom_call" | custom-call | flops 3221225472 | bytes 6291456 | tf_op jit(solution)/shard_map/key_pass/pallas_call | solution.py:205
  116.8 2.6 %collective-permute-done.22.grad_ref = bf16[4,3,272,128]{3,2,1,0:T(8,128)(2,1)} collective-permute-done((bf16[4,3,272,128]{3,2,1,0:T(8,128)(2,1)S(1)}, bf16[4,3,272,128]{3,2,1,0:T(8,128)(2,1)}, u32[]{:S(2)}, u32[]{:S(2)}) %collective-permute-start.22) | collective-permute-done | bytes 835616 | tf_op jit(solution)/shard_map/ppermute | solution.py:299
  120.7 4.3 %query_pass.5.rest_0_ = f32[4,3,256,128]{3,2,1,0:T(8,128)S(1)} custom-call(s32[5]{0:T(128)S(1)} %get-tuple-element.69.meta_ref, bf16[4,3,256,128]{3,2,1,0:T(8,128)(2,1)S(1)} %pad_maximum_fusion.2.query_ref, bf16[4,3,272,128]{3,2,1,0:T(8,128)(2,1)S(1)} %pad_maximum_fusion.1.grad_ref, bf16[4,3,256,128]{3,2,1,0:T(8,128)(2,1)} %collective-permute-done.10.key_ref, ...), custom_call_target="tpu_custom_call" | custom-call | flops 2415919104 | bytes 6291456 | tf_op jit(solution)/shard_map/query_pass/pallas_call | solution.py:205
  126.1 9.9 %collective-permute-done.20.query_ref = bf16[4,3,256,128]{3,2,1,0:T(8,128)(2,1)} collective-permute-done((bf16[4,3,256,128]{3,2,1,0:T(8,128)(2,1)}, bf16[4,3,256,128]{3,2,1,0:T(8,128)(2,1)}, u32[]{:S(2)}, u32[]{:S(2)}) %collective-permute-start.20) | collective-permute-done | bytes 786464 | tf_op jit(solution)/shard_map/ppermute | solution.py:299
  137.5 4.3 %query_pass.6.rest_0_ = f32[4,3,256,128]{3,2,1,0:T(8,128)S(1)} custom-call(s32[5]{0:T(128)S(1)} %get-tuple-element.68.meta_ref, bf16[4,3,256,128]{3,2,1,0:T(8,128)(2,1)S(1)} %pad_maximum_fusion.2.query_ref, bf16[4,3,272,128]{3,2,1,0:T(8,128)(2,1)S(1)} %pad_maximum_fusion.1.grad_ref, bf16[4,3,256,128]{3,2,1,0:T(8,128)(2,1)} %collective-permute-done.11.key_ref, ...), custom_call_target="tpu_custom_call" | custom-call | flops 2415919104 | bytes 6291456 | tf_op jit(solution)/shard_map/query_pass/pallas_call | solution.py:205
  143.3 1.8 collective-permute-start.17
  145.2 12.1 %collective-permute-done.23.grad_ref = bf16[4,3,272,128]{3,2,1,0:T(8,128)(2,1)S(1)} collective-permute-done((bf16[4,3,272,128]{3,2,1,0:T(8,128)(2,1)}, bf16[4,3,272,128]{3,2,1,0:T(8,128)(2,1)S(1)}, u32[]{:S(2)}, u32[]{:S(2)}) %collective-permute-start.23) | collective-permute-done | bytes 835616 | tf_op jit(solution)/shard_map/ppermute | solution.py:299
  158.5 12.1 %key_pass.5 = (f32[4,3,256,128]{3,2,1,0:T(8,128)S(1)}, f32[4,3,256,128]{3,2,1,0:T(8,128)}) custom-call(s32[5]{0:T(128)S(1)} %get-tuple-element.67.meta_ref, bf16[4,3,256,128]{3,2,1,0:T(8,128)(2,1)} %collective-permute-done.19.query_ref, bf16[4,3,272,128]{3,2,1,0:T(8,128)(2,1)} %collective-permute-done.22.grad_ref, ...), custom_call_target="tpu_custom_call" | custom-call | flops 3221225472 | bytes 6291456 | tf_op jit(solution)/shard_map/key_pass/pallas_call | solution.py:205
  172.7 12.0 %key_pass.6 = (f32[4,3,256,128]{3,2,1,0:T(8,128)S(1)}, f32[4,3,256,128]{3,2,1,0:T(8,128)}) custom-call(s32[5]{0:T(128)S(1)} %get-tuple-element.71.meta_ref, bf16[4,3,256,128]{3,2,1,0:T(8,128)(2,1)} %collective-permute-done.20.query_ref, bf16[4,3,272,128]{3,2,1,0:T(8,128)(2,1)S(1)} %collective-permute-done.23.grad_ref, ...), custom_call_target="tpu_custom_call" | custom-call | flops 3221225472 | bytes 6291456 | tf_op jit(solution)/shard_map/key_pass/pallas_call | solution.py:205
  185.8 5.8 %collective-permute-done.24.grad_ref = bf16[4,3,272,128]{3,2,1,0:T(8,128)(2,1)S(1)} collective-permute-done((bf16[4,3,272,128]{3,2,1,0:T(8,128)(2,1)S(1)}, bf16[4,3,272,128]{3,2,1,0:T(8,128)(2,1)S(1)}, u32[]{:S(2)}, u32[]{:S(2)}) %collective-permute-start.24) | collective-permute-done | bytes 835616 | tf_op jit(solution)/shard_map/ppermute | solution.py:299
  191.7 11.3 %key_pass.7 = (bf16[4,3,256,128]{3,2,1,0:T(8,128)(2,1)S(1)}, bf16[4,3,256,128]{3,2,1,0:T(8,128)(2,1)S(1)}) custom-call(s32[5]{0:T(128)S(1)} %get-tuple-element.72.meta_ref, bf16[4,3,256,128]{3,2,1,0:T(8,128)(2,1)S(1)} %collective-permute-done.21.query_ref, bf16[4,3,272,128]{3,2,1,0:T(8,128)(2,1)S(1)} %collective-permute-done.24.grad_ref, ...), custom_call_target="tpu_custom_call" | custom-call | flops 3221225472 | bytes 6291456 | tf_op jit(solution)/shard_map/key_pass/pallas_call | solution.py:205
  206.9 3.9 %collective-permute-done.29 = bf16[3,256,128]{2,1,0:T(8,128)(2,1)S(1)} collective-permute-done((bf16[3,256,128]{2,1,0:T(8,128)(2,1)S(1)}, bf16[3,256,128]{2,1,0:T(8,128)(2,1)S(1)}, u32[]{:S(2)}, u32[]{:S(2)}) %collective-permute-start.29) | collective-permute-done | bytes 196640 | tf_op jit(solution)/shard_map/ppermute | solution.py:245
  210.8 3.3 %collective-permute-done.30 = bf16[3,256,128]{2,1,0:T(8,128)(2,1)S(1)} collective-permute-done((bf16[3,256,128]{2,1,0:T(8,128)(2,1)S(1)}, bf16[3,256,128]{2,1,0:T(8,128)(2,1)S(1)}, u32[]{:S(2)}, u32[]{:S(2)}) %collective-permute-start.30) | collective-permute-done | bytes 196640 | tf_op jit(solution)/shard_map/ppermute | solution.py:245
  214.3 4.9 %collective-permute-done.26 = bf16[3,256,128]{2,1,0:T(8,128)(2,1)S(1)} collective-permute-done((bf16[3,256,128]{2,1,0:T(8,128)(2,1)S(1)}, bf16[3,256,128]{2,1,0:T(8,128)(2,1)S(1)}, u32[]{:S(2)}, u32[]{:S(2)}) %collective-permute-start.26) | collective-permute-done | bytes 196640 | tf_op jit(solution)/shard_map/ppermute | solution.py:245
  219.3 3.3 %collective-permute-done.27 = bf16[3,256,128]{2,1,0:T(8,128)(2,1)S(1)} collective-permute-done((bf16[3,256,128]{2,1,0:T(8,128)(2,1)S(1)}, bf16[3,256,128]{2,1,0:T(8,128)(2,1)S(1)}, u32[]{:S(2)}, u32[]{:S(2)}) %collective-permute-start.27) | collective-permute-done | bytes 196640 | tf_op jit(solution)/shard_map/ppermute | solution.py:245
  (89 shorter events, 37.1 us)
Async XLA Ops:
  0.7 48.9 %collective-permute-start.3 = (bf16[256,2560]{1,0:T(8,128)(2,1)}, bf16[256,2560]{1,0:T(8,128)(2,1)}, u32[]{:S(2)}, u32[]{:S(2)}) collective-permute-start(bf16[256,2560]{1,0:T(8,128)(2,1)} %param.11), channel_id=1, source_target_pairs={{0,1},{1,0},{2,3},{3,2},{4,5},{5,4},{6,7},{7,6},{8,9},{9,8},{10,11... | collective-permute-start | bytes 3932168 | tf_op jit(solution)/shard_map/ppermute | solution.py:253
  13.7 7.8 %collective-permute-start.1 = (bf16[3,256,128]{2,1,0:T(8,128)(2,1)S(1)}, bf16[3,256,128]{2,1,0:T(8,128)(2,1)S(1)}, u32[]{:S(2)}, u32[]{:S(2)}) collective-permute-start(bf16[3,256,128]{2,1,0:T(8,128)(2,1)S(1)} %get-tuple-element.65), channel_id=1, source_target_pairs={{0,4},{2,6},{4,0},{6,2},{8,12},{10,14},{12,8},{14,10},{16,20},{18,... | collective-permute-start | bytes 589832 | tf_op jit(solution)/shard_map/ppermute | solution.py:245
  15.2 9.6 %collective-permute-start.2 = (bf16[3,256,128]{2,1,0:T(8,128)(2,1)S(1)}, bf16[3,256,128]{2,1,0:T(8,128)(2,1)}, u32[]{:S(2)}, u32[]{:S(2)}) collective-permute-start(bf16[3,256,128]{2,1,0:T(8,128)(2,1)S(1)} %get-tuple-element.64), channel_id=1, source_target_pairs={{0,6},{2,4},{4,2},{6,0},{8,14},{10,12},{12,10},{14,8},{16,22},{18,... | collective-permute-start | bytes 589832 | tf_op jit(solution)/shard_map/ppermute | solution.py:245
  15.7 14.6 %collective-permute-start.7 = (bf16[2,3,256,128]{3,2,1,0:T(8,128)(2,1)S(1)}, bf16[2,3,256,128]{3,2,1,0:T(8,128)(2,1)S(1)}, u32[]{:S(2)}, u32[]{:S(2)}) collective-permute-start(bf16[2,3,256,128]{3,2,1,0:T(8,128)(2,1)S(1)} %get-tuple-element.24), channel_id=1, source_target_pairs={{0,2},{2,0},{4,6},{6,4},{8,10},{10,8},{12,14},{14,12},{16,18},{18,... | collective-permute-start | bytes 1179656 | tf_op jit(solution)/shard_map/ppermute | solution.py:245
  16.4 17.7 %collective-permute-start.8 = (bf16[2,3,256,128]{3,2,1,0:T(8,128)(2,1)S(1)}, bf16[2,3,256,128]{3,2,1,0:T(8,128)(2,1)S(1)}, u32[]{:S(2)}, u32[]{:S(2)}) collective-permute-start(bf16[2,3,256,128]{3,2,1,0:T(8,128)(2,1)S(1)} %get-tuple-element.26), channel_id=1, source_target_pairs={{0,4},{2,6},{4,0},{6,2},{8,12},{10,14},{12,8},{14,10},{16,20},{18,... | collective-permute-start | bytes 1179656 | tf_op jit(solution)/shard_map/ppermute | solution.py:245
  21.5 18.6 %collective-permute-start.9 = (bf16[2,3,256,128]{3,2,1,0:T(8,128)(2,1)S(1)}, bf16[2,3,256,128]{3,2,1,0:T(8,128)(2,1)}, u32[]{:S(2)}, u32[]{:S(2)}) collective-permute-start(bf16[2,3,256,128]{3,2,1,0:T(8,128)(2,1)S(1)} %get-tuple-element.25), channel_id=1, source_target_pairs={{0,6},{2,4},{4,2},{6,0},{8,14},{10,12},{12,10},{14,8},{16,22},{18,... | collective-permute-start | bytes 1179656 | tf_op jit(solution)/shard_map/ppermute | solution.py:245
  24.7 2.5 %collective-permute-start = (bf16[3,256,128]{2,1,0:T(8,128)(2,1)}, bf16[3,256,128]{2,1,0:T(8,128)(2,1)S(1)}, u32[]{:S(2)}, u32[]{:S(2)}) collective-permute-start(bf16[3,256,128]{2,1,0:T(8,128)(2,1)} %get-tuple-element.66), channel_id=1, source_target_pairs={{0,2},{2,0},{4,6},{6,4},{8,10},{10,8},{12,14},{14,12},{16,18},{18,... | collective-permute-start | bytes 589832 | tf_op jit(solution)/shard_map/ppermute | solution.py:245
  29.0 65.0 %collective-permute-start.19 = (bf16[4,3,256,128]{3,2,1,0:T(8,128)(2,1)S(1)}, bf16[4,3,256,128]{3,2,1,0:T(8,128)(2,1)}, u32[]{:S(2)}, u32[]{:S(2)}) collective-permute-start(bf16[4,3,256,128]{3,2,1,0:T(8,128)(2,1)S(1)} %pad_maximum_fusion.2.query_ref), channel_id=1, source_target_pairs={{8,0},{10,2},{12,4},{14,6},{16,8},{18,10},{20,12},{22,14},{24,16},... | collective-permute-start | bytes 2359304 | tf_op jit(solution)/shard_map/ppermute | solution.py:299
  41.5 32.8 %collective-permute-start.10 = (bf16[4,3,256,128]{3,2,1,0:T(8,128)(2,1)S(1)}, bf16[4,3,256,128]{3,2,1,0:T(8,128)(2,1)}, u32[]{:S(2)}, u32[]{:S(2)}) collective-permute-start(bf16[4,3,256,128]{3,2,1,0:T(8,128)(2,1)S(1)} %get-tuple-element.22.key_ref), channel_id=1, source_target_pairs={{0,8},{2,10},{4,12},{6,14},{8,16},{10,18},{12,20},{14,22},{16,24},... | collective-permute-start | bytes 2359304 | tf_op jit(solution)/shard_map/ppermute | solution.py:298
  46.0 33.7 %collective-permute-start.13 = (bf16[4,3,256,128]{3,2,1,0:T(8,128)(2,1)S(1)}, bf16[4,3,256,128]{3,2,1,0:T(8,128)(2,1)}, u32[]{:S(2)}, u32[]{:S(2)}) collective-permute-start(bf16[4,3,256,128]{3,2,1,0:T(8,128)(2,1)S(1)} %get-tuple-element.21.value_ref), channel_id=1, source_target_pairs={{0,8},{2,10},{4,12},{6,14},{8,16},{10,18},{12,20},{14,22},{16,24},... | collective-permute-start | bytes 2359304 | tf_op jit(solution)/shard_map/ppermute | solution.py:298
  72.2 21.7 %copy-start.10 = (s32[4]{0:T(128)S(1)}, s32[4]{0:T(128)}, u32[]{:S(2)}) copy-start(s32[4]{0:T(128)} %copy-done.9) | copy-start | bytes 52
  73.5 8.4 %collective-permute-start.4 = (bf16[3,272,128]{2,1,0:T(8,128)(2,1)S(1)}, bf16[3,272,128]{2,1,0:T(8,128)(2,1)S(1)}, u32[]{:S(2)}, u32[]{:S(2)}) collective-permute-start(bf16[3,272,128]{2,1,0:T(8,128)(2,1)S(1)} %get-tuple-element.30), channel_id=1, source_target_pairs={{0,2},{2,0},{4,6},{6,4},{8,10},{10,8},{12,14},{14,12},{16,18},{18,... | collective-permute-start | bytes 626696 | tf_op jit(solution)/shard_map/ppermute | solution.py:245
  74.2 21.2 %collective-permute-start.11 = (bf16[4,3,256,128]{3,2,1,0:T(8,128)(2,1)}, bf16[4,3,256,128]{3,2,1,0:T(8,128)(2,1)}, u32[]{:S(2)}, u32[]{:S(2)}) collective-permute-start(bf16[4,3,256,128]{3,2,1,0:T(8,128)(2,1)} %collective-permute-done.10.key_ref), channel_id=1, source_target_pairs={{8,16},{10,18},{12,20},{14,22},{16,24},{18,26},{20,28},{22,30},{9,... | collective-permute-start | bytes 2359304 | tf_op jit(solution)/shard_map/ppermute | solution.py:298
  79.6 16.5 %collective-permute-start.14 = (bf16[4,3,256,128]{3,2,1,0:T(8,128)(2,1)}, bf16[4,3,256,128]{3,2,1,0:T(8,128)(2,1)}, u32[]{:S(2)}, u32[]{:S(2)}) collective-permute-start(bf16[4,3,256,128]{3,2,1,0:T(8,128)(2,1)} %collective-permute-done.13.value_ref), channel_id=1, source_target_pairs={{8,16},{10,18},{12,20},{14,22},{16,24},{18,26},{20,28},{22,30},{9,... | collective-permute-start | bytes 2359304 | tf_op jit(solution)/shard_map/ppermute | solution.py:298
  81.2 8.0 %collective-permute-start.5 = (bf16[3,272,128]{2,1,0:T(8,128)(2,1)S(1)}, bf16[3,272,128]{2,1,0:T(8,128)(2,1)S(1)}, u32[]{:S(2)}, u32[]{:S(2)}) collective-permute-start(bf16[3,272,128]{2,1,0:T(8,128)(2,1)S(1)} %get-tuple-element.29), channel_id=1, source_target_pairs={{0,4},{2,6},{4,0},{6,2},{8,12},{10,14},{12,8},{14,10},{16,20},{18,... | collective-permute-start | bytes 626696 | tf_op jit(solution)/shard_map/ppermute | solution.py:245
  82.0 10.5 %collective-permute-start.6 = (bf16[3,272,128]{2,1,0:T(8,128)(2,1)S(1)}, bf16[3,272,128]{2,1,0:T(8,128)(2,1)S(1)}, u32[]{:S(2)}, u32[]{:S(2)}) collective-permute-start(bf16[3,272,128]{2,1,0:T(8,128)(2,1)S(1)} %get-tuple-element.28), channel_id=1, source_target_pairs={{0,6},{2,4},{4,2},{6,0},{8,14},{10,12},{12,10},{14,8},{16,22},{18,... | collective-permute-start | bytes 626696 | tf_op jit(solution)/shard_map/ppermute | solution.py:245
  92.6 26.8 %collective-permute-start.22 = (bf16[4,3,272,128]{3,2,1,0:T(8,128)(2,1)S(1)}, bf16[4,3,272,128]{3,2,1,0:T(8,128)(2,1)}, u32[]{:S(2)}, u32[]{:S(2)}) collective-permute-start(bf16[4,3,272,128]{3,2,1,0:T(8,128)(2,1)S(1)} %pad_maximum_fusion.1.grad_ref), channel_id=1, source_target_pairs={{8,0},{10,2},{12,4},{14,6},{16,8},{18,10},{20,12},{22,14},{24,16},... | collective-permute-start | bytes 2506760 | tf_op jit(solution)/shard_map/ppermute | solution.py:299
  94.0 42.0 %collective-permute-start.20 = (bf16[4,3,256,128]{3,2,1,0:T(8,128)(2,1)}, bf16[4,3,256,128]{3,2,1,0:T(8,128)(2,1)}, u32[]{:S(2)}, u32[]{:S(2)}) collective-permute-start(bf16[4,3,256,128]{3,2,1,0:T(8,128)(2,1)} %collective-permute-done.19.query_ref), channel_id=1, source_target_pairs={{8,0},{10,2},{12,4},{14,6},{16,8},{18,10},{20,12},{22,14},{9,1},{1... | collective-permute-start | bytes 2359304 | tf_op jit(solution)/shard_map/ppermute | solution.py:299
  95.4 46.3 %collective-permute-start.12 = (bf16[4,3,256,128]{3,2,1,0:T(8,128)(2,1)}, bf16[4,3,256,128]{3,2,1,0:T(8,128)(2,1)S(1)}, u32[]{:S(2)}, u32[]{:S(2)}) collective-permute-start(bf16[4,3,256,128]{3,2,1,0:T(8,128)(2,1)} %collective-permute-done.11.key_ref), channel_id=1, source_target_pairs={{16,24},{18,26},{20,28},{22,30},{17,25},{19,27},{21,29},{23,31}} | collective-permute-start | bytes 2359304 | tf_op jit(solution)/shard_map/ppermute | solution.py:298
  96.1 45.6 %collective-permute-start.15 = (bf16[4,3,256,128]{3,2,1,0:T(8,128)(2,1)}, bf16[4,3,256,128]{3,2,1,0:T(8,128)(2,1)S(1)}, u32[]{:S(2)}, u32[]{:S(2)}) collective-permute-start(bf16[4,3,256,128]{3,2,1,0:T(8,128)(2,1)} %collective-permute-done.14.value_ref), channel_id=1, source_target_pairs={{16,24},{18,26},{20,28},{22,30},{17,25},{19,27},{21,29},{23,31}} | collective-permute-start | bytes 2359304 | tf_op jit(solution)/shard_map/ppermute | solution.py:298
  119.4 37.9 %collective-permute-start.23 = (bf16[4,3,272,128]{3,2,1,0:T(8,128)(2,1)}, bf16[4,3,272,128]{3,2,1,0:T(8,128)(2,1)S(1)}, u32[]{:S(2)}, u32[]{:S(2)}) collective-permute-start(bf16[4,3,272,128]{3,2,1,0:T(8,128)(2,1)} %collective-permute-done.22.grad_ref), channel_id=1, source_target_pairs={{8,0},{10,2},{12,4},{14,6},{16,8},{18,10},{20,12},{22,14},{9,1},{1... | collective-permute-start | bytes 2506760 | tf_op jit(solution)/shard_map/ppermute | solution.py:299
  136.0 49.9 %collective-permute-start.21 = (bf16[4,3,256,128]{3,2,1,0:T(8,128)(2,1)}, bf16[4,3,256,128]{3,2,1,0:T(8,128)(2,1)S(1)}, u32[]{:S(2)}, u32[]{:S(2)}) collective-permute-start(bf16[4,3,256,128]{3,2,1,0:T(8,128)(2,1)} %collective-permute-done.20.query_ref), channel_id=1, source_target_pairs={{8,0},{10,2},{12,4},{14,6},{9,1},{11,3},{13,5},{15,7}} | collective-permute-start | bytes 2359304 | tf_op jit(solution)/shard_map/ppermute | solution.py:299
  143.2 27.4 %collective-permute-start.16 = (bf16[3,256,128]{2,1,0:T(8,128)(2,1)S(1)}, bf16[3,256,128]{2,1,0:T(8,128)(2,1)S(1)}, u32[]{:S(2)}, u32[]{:S(2)}) collective-permute-start(bf16[3,256,128]{2,1,0:T(8,128)(2,1)S(1)} %get-tuple-element.54), channel_id=1, source_target_pairs={{0,2},{2,0},{4,6},{6,4},{8,10},{10,8},{12,14},{14,12},{16,18},{18,... | collective-permute-start | bytes 589832 | tf_op jit(solution)/shard_map/ppermute | solution.py:245
  143.3 27.3 %collective-permute-start.17 = (bf16[3,256,128]{2,1,0:T(8,128)(2,1)S(1)}, bf16[3,256,128]{2,1,0:T(8,128)(2,1)S(1)}, u32[]{:S(2)}, u32[]{:S(2)}) collective-permute-start(bf16[3,256,128]{2,1,0:T(8,128)(2,1)S(1)} %get-tuple-element.53), channel_id=1, source_target_pairs={{0,4},{2,6},{4,0},{6,2},{8,12},{10,14},{12,8},{14,10},{16,20},{18,... | collective-permute-start | bytes 589832 | tf_op jit(solution)/shard_map/ppermute | solution.py:245
  145.1 25.5 %collective-permute-start.18 = (bf16[3,256,128]{2,1,0:T(8,128)(2,1)S(1)}, bf16[3,256,128]{2,1,0:T(8,128)(2,1)S(1)}, u32[]{:S(2)}, u32[]{:S(2)}) collective-permute-start(bf16[3,256,128]{2,1,0:T(8,128)(2,1)S(1)} %get-tuple-element.52), channel_id=1, source_target_pairs={{0,6},{2,4},{4,2},{6,0},{8,14},{10,12},{12,10},{14,8},{16,22},{18,... | collective-permute-start | bytes 589832 | tf_op jit(solution)/shard_map/ppermute | solution.py:245
  157.2 34.4 %collective-permute-start.24 = (bf16[4,3,272,128]{3,2,1,0:T(8,128)(2,1)S(1)}, bf16[4,3,272,128]{3,2,1,0:T(8,128)(2,1)S(1)}, u32[]{:S(2)}, u32[]{:S(2)}) collective-permute-start(bf16[4,3,272,128]{3,2,1,0:T(8,128)(2,1)S(1)} %collective-permute-done.23.grad_ref), channel_id=1, source_target_pairs={{8,0},{10,2},{12,4},{14,6},{9,1},{11,3},{13,5},{15,7}} | collective-permute-start | bytes 2506760 | tf_op jit(solution)/shard_map/ppermute | solution.py:299
  203.0 3.6 %collective-permute-start.28 = (bf16[3,256,128]{2,1,0:T(8,128)(2,1)S(1)}, bf16[3,256,128]{2,1,0:T(8,128)(2,1)S(1)}, u32[]{:S(2)}, u32[]{:S(2)}) collective-permute-start(bf16[3,256,128]{2,1,0:T(8,128)(2,1)S(1)} %get-tuple-element.38), channel_id=1, source_target_pairs={{0,2},{2,0},{4,6},{6,4},{8,10},{10,8},{12,14},{14,12},{16,18},{18,... | collective-permute-start | bytes 589832 | tf_op jit(solution)/shard_map/ppermute | solution.py:245
  203.1 7.8 %collective-permute-start.29 = (bf16[3,256,128]{2,1,0:T(8,128)(2,1)S(1)}, bf16[3,256,128]{2,1,0:T(8,128)(2,1)S(1)}, u32[]{:S(2)}, u32[]{:S(2)}) collective-permute-start(bf16[3,256,128]{2,1,0:T(8,128)(2,1)S(1)} %get-tuple-element.37), channel_id=1, source_target_pairs={{0,4},{2,6},{4,0},{6,2},{8,12},{10,14},{12,8},{14,10},{16,20},{18,... | collective-permute-start | bytes 589832 | tf_op jit(solution)/shard_map/ppermute | solution.py:245
  204.3 9.9 %collective-permute-start.30 = (bf16[3,256,128]{2,1,0:T(8,128)(2,1)S(1)}, bf16[3,256,128]{2,1,0:T(8,128)(2,1)S(1)}, u32[]{:S(2)}, u32[]{:S(2)}) collective-permute-start(bf16[3,256,128]{2,1,0:T(8,128)(2,1)S(1)} %get-tuple-element.36), channel_id=1, source_target_pairs={{0,6},{2,4},{4,2},{6,0},{8,14},{10,12},{12,10},{14,8},{16,22},{18,... | collective-permute-start | bytes 589832 | tf_op jit(solution)/shard_map/ppermute | solution.py:245
  205.0 9.3 %collective-permute-start.25 = (bf16[3,256,128]{2,1,0:T(8,128)(2,1)S(1)}, bf16[3,256,128]{2,1,0:T(8,128)(2,1)S(1)}, u32[]{:S(2)}, u32[]{:S(2)}) collective-permute-start(bf16[3,256,128]{2,1,0:T(8,128)(2,1)S(1)} %get-tuple-element.46), channel_id=1, source_target_pairs={{0,2},{2,0},{4,6},{6,4},{8,10},{10,8},{12,14},{14,12},{16,18},{18,... | collective-permute-start | bytes 589832 | tf_op jit(solution)/shard_map/ppermute | solution.py:245
  205.4 13.9 %collective-permute-start.26 = (bf16[3,256,128]{2,1,0:T(8,128)(2,1)S(1)}, bf16[3,256,128]{2,1,0:T(8,128)(2,1)S(1)}, u32[]{:S(2)}, u32[]{:S(2)}) collective-permute-start(bf16[3,256,128]{2,1,0:T(8,128)(2,1)S(1)} %get-tuple-element.45), channel_id=1, source_target_pairs={{0,4},{2,6},{4,0},{6,2},{8,12},{10,14},{12,8},{14,10},{16,20},{18,... | collective-permute-start | bytes 589832 | tf_op jit(solution)/shard_map/ppermute | solution.py:245
  206.6 16.0 %collective-permute-start.27 = (bf16[3,256,128]{2,1,0:T(8,128)(2,1)S(1)}, bf16[3,256,128]{2,1,0:T(8,128)(2,1)S(1)}, u32[]{:S(2)}, u32[]{:S(2)}) collective-permute-start(bf16[3,256,128]{2,1,0:T(8,128)(2,1)S(1)} %get-tuple-element.44), channel_id=1, source_target_pairs={{0,6},{2,4},{4,2},{6,0},{8,14},{10,12},{12,10},{14,8},{16,22},{18,... | collective-permute-start | bytes 589832 | tf_op jit(solution)/shard_map/ppermute | solution.py:245
  (10 other events, 64.4 us)
